TPU v7x, 32 devices: a whole 2x2x4 slice. The times are simulated.
32 devices in a mesh: groups: 2 (over x), ctx: 8 (over z, y), dp: 2 (over core).
Axes of the slice: x: 2, y: 2, z: 4, core: 2. Of those that a mesh axis runs over, the one named last changes fastest.
Arguments:
- inputs: bfloat16 [4, 4096, 256], P(('groups', 'dp'), 'ctx'), parts along dimension 0, may hold values from -6 to 6
- value_weight: bfloat16 [256, 256], replicated, may hold values from -0.375 to 0.375
- gate_weight: bfloat16 [256, 256], replicated, may hold values from -0.375 to 0.375
- output_weight: bfloat16 [256, 256], replicated, may hold values from -0.375 to 0.375
- filters: bfloat16 [4096, 256], P('ctx'), may hold values from -0.09375 to 0.09375
- cotangent: bfloat16 [4, 4096, 256], P(('groups', 'dp'), 'ctx'), parts along dimension 0, may hold values from -6 to 6
Outputs:
- input_grad: bfloat16 [4, 4096, 256], P(('groups', 'dp'), 'ctx'), parts along dimension 0
- proj_grads: float32 [6, 256, 256], P('groups', 'ctx'), parts along dimension 0
- filter_grads: float32 [8192, 256], P(('groups', 'ctx')), parts along dimension 0
There are 2 independent parts, one for each index of `groups`. A program takes and returns all parts, laid end to end along the dimension named above; an argument that names none is the same for every part. Nothing has to cross between parts.
All inputs are finite; a program needn't handle non-finite values.
Results may differ from a plain program's by a relative error of at most 0.0057.
Values may be sent and summed in bfloat16 or wider, within the bound.
A program may use at most 64 MiB of HBM per device.

v0:
```python
import math
import jax
import jax.numpy as jnp
from jax import lax
from jax.sharding import PartitionSpec as P


def phase_table(left, right, modulus, sign):
    product = left[:, None] * right[None, :] % modulus
    return sign * (2.0 * math.pi / modulus) * product.astype(jnp.float32)


def dft_matrix(size, sign):
    counter = jnp.arange(size, dtype=jnp.int32)
    phase = phase_table(counter, counter, size, sign)
    return (jnp.cos(phase), jnp.sin(phase))


def apply_left(matrix, field):
    return jnp.tensordot(matrix, field, axes=(1, 0), precision=lax.Precision.HIGHEST)


def mix_first(cos_table, sin_table, real_part, imag_part):
    new_real = apply_left(cos_table, real_part) - apply_left(sin_table, imag_part)
    new_imag = apply_left(cos_table, imag_part) + apply_left(sin_table, real_part)
    return (new_real, new_imag)


def apply_middle(matrix, field):
    return jnp.einsum("kb,abw->akw", matrix, field, precision=lax.Precision.HIGHEST)


def mix_second(cos_table, sin_table, real_part, imag_part):
    new_real = apply_middle(cos_table, real_part) - apply_middle(sin_table, imag_part)
    new_imag = apply_middle(cos_table, imag_part) + apply_middle(sin_table, real_part)
    return (new_real, new_imag)


def rotate(real_part, imag_part, cos_part, sin_part):
    return (
        real_part * cos_part - imag_part * sin_part,
        real_part * sin_part + imag_part * cos_part,
    )


def local_dft(real_part, imag_part, sign):
    length = real_part.shape[0]
    columns = real_part.shape[1]
    outer = 32
    inner = length // outer
    real_part = real_part.reshape(outer, inner, columns)
    imag_part = imag_part.reshape(outer, inner, columns)
    cos_table, sin_table = dft_matrix(outer, sign)
    real_part, imag_part = mix_first(cos_table, sin_table, real_part, imag_part)
    phase = phase_table(
        jnp.arange(outer, dtype=jnp.int32), jnp.arange(inner, dtype=jnp.int32), length, sign
    )[:, :, None]
    real_part, imag_part = rotate(real_part, imag_part, jnp.cos(phase), jnp.sin(phase))
    cos_table, sin_table = dft_matrix(inner, sign)
    real_part, imag_part = mix_second(cos_table, sin_table, real_part, imag_part)
    real_part = real_part.transpose(1, 0, 2).reshape(length, columns)
    imag_part = imag_part.transpose(1, 0, 2).reshape(length, columns)
    return (real_part, imag_part)


def forward_transform(stacked):
    count = lax.axis_size("ctx")
    place = lax.axis_index("ctx")
    tok_rows = stacked.shape[0]
    total = count * tok_rows
    piece = tok_rows // count
    moved = lax.all_to_all(stacked[None], "ctx", split_axis=1, concat_axis=0, tiled=True)
    real_rows = moved.astype(jnp.float32)
    cos_table, sin_table = dft_matrix(count, -1.0)
    real_part = apply_left(cos_table, real_rows)
    imag_part = apply_left(sin_table, real_rows)
    row_index = place * piece + jnp.arange(piece, dtype=jnp.int32)
    phase = phase_table(jnp.arange(count, dtype=jnp.int32), row_index, total, -1.0)[:, :, None]
    real_part, imag_part = rotate(real_part, imag_part, jnp.cos(phase), jnp.sin(phase))
    real_part, imag_part = (
        lax.all_to_all(real_part, "ctx", split_axis=0, concat_axis=1, tiled=True),
        lax.all_to_all(imag_part, "ctx", split_axis=0, concat_axis=1, tiled=True),
    )
    return local_dft(real_part[0], imag_part[0], -1.0)


def inverse_transform(real_part, imag_part):
    count = lax.axis_size("ctx")
    place = lax.axis_index("ctx")
    tok_rows = real_part.shape[0]
    total = count * tok_rows
    real_part, imag_part = local_dft(real_part, imag_part, 1.0)
    product = place * jnp.arange(tok_rows, dtype=jnp.int32) % total
    phase = (2.0 * math.pi / total * product.astype(jnp.float32))[:, None]
    real_part, imag_part = rotate(real_part, imag_part, jnp.cos(phase), jnp.sin(phase))
    real_part, imag_part = (
        lax.all_to_all(real_part[None], "ctx", split_axis=1, concat_axis=0, tiled=True),
        lax.all_to_all(imag_part[None], "ctx", split_axis=1, concat_axis=0, tiled=True),
    )
    cos_table, sin_table = dft_matrix(count, 1.0)
    rows_part = apply_left(cos_table, real_part) - apply_left(sin_table, imag_part)
    returned = lax.all_to_all(rows_part, "ctx", split_axis=0, concat_axis=1, tiled=True)
    return returned[0] * (1.0 / total)


def contract_rows(left_rows, right_rows):
    return lax.dot_general(
        left_rows, right_rows, (((0,), (0,)), ((), ())), preferred_element_type=jnp.float32
    )


def times_transpose(left_rows, weight):
    return lax.dot_general(
        left_rows, weight, (((1,), (1,)), ((), ())), preferred_element_type=jnp.float32
    )


def local(inputs, value_weight, gate_weight, output_weight, filters, cotangent):
    token_rows = inputs[0]
    upstream = cotangent[0]
    tok_rows = token_rows.shape[0]
    width = token_rows.shape[1]
    value_act = jnp.dot(token_rows, value_weight, preferred_element_type=jnp.float32).astype(
        jnp.bfloat16
    )
    gate_act = jnp.dot(token_rows, gate_weight, preferred_element_type=jnp.float32)
    d_gated = times_transpose(upstream, output_weight)
    d_mixed = (d_gated * gate_act).astype(jnp.bfloat16)
    share = width // lax.axis_size("dp")
    kernel_part = lax.dynamic_slice_in_dim(filters, lax.axis_index("dp") * share, share, 1)
    spec_real, spec_imag = forward_transform(
        jnp.concatenate([value_act, d_mixed, kernel_part], axis=1)
    )
    value_real = spec_real[:, :width]
    value_imag = spec_imag[:, :width]
    grad_real = spec_real[:, width : 2 * width]
    grad_imag = spec_imag[:, width : 2 * width]
    kernel_real = spec_real[:, 2 * width :]
    kernel_imag = spec_imag[:, 2 * width :]
    kernel_real, kernel_imag = (
        lax.all_gather(kernel_real, "dp", axis=1, tiled=True),
        lax.all_gather(kernel_imag, "dp", axis=1, tiled=True),
    )
    mixed_real = value_real * kernel_real - value_imag * kernel_imag
    mixed_imag = value_real * kernel_imag + value_imag * kernel_real
    back_real = grad_real * kernel_real + grad_imag * kernel_imag
    back_imag = grad_imag * kernel_real - grad_real * kernel_imag
    corr_real = grad_real * value_real + grad_imag * value_imag
    corr_imag = grad_imag * value_real - grad_real * value_imag
    grad_scale = 1.0 / math.sqrt(lax.axis_size("dp") * lax.axis_size("ctx") * tok_rows)
    rows_all = inverse_transform(
        jnp.concatenate([mixed_real, back_real, corr_real], axis=1),
        jnp.concatenate([mixed_imag, back_imag, corr_imag], axis=1),
    )
    mixed_act = rows_all[:, :width]
    d_value = rows_all[:, width : 2 * width].astype(jnp.bfloat16)
    filter_terms = rows_all[:, 2 * width :] * grad_scale
    gated = (gate_act * mixed_act).astype(jnp.bfloat16)
    d_gate = (d_gated * mixed_act).astype(jnp.bfloat16)
    input_rows = times_transpose(d_value, value_weight) + times_transpose(d_gate, gate_weight)
    input_grad = input_rows.astype(jnp.bfloat16)[None]
    proj_terms = (
        jnp.stack(
            [
                contract_rows(token_rows, d_value),
                contract_rows(token_rows, d_gate),
                contract_rows(gated, upstream),
            ],
            axis=0,
        )
        * grad_scale
    )
    proj_part = lax.psum_scatter(proj_terms, "ctx", scatter_dimension=1, tiled=True)
    proj_grads, filter_grads = lax.psum((proj_part, filter_terms), "dp")
    return (input_grad, proj_grads, filter_grads)


def solution(mesh):
    return jax.shard_map(
        local,
        mesh=mesh,
        in_specs=(
            P(("groups", "dp"), "ctx", None),
            P(),
            P(),
            P(),
            P("ctx", None),
            P(("groups", "dp"), "ctx", None),
        ),
        out_specs=(
            P(("groups", "dp"), "ctx", None),
            P("groups", "ctx", None),
            P(("groups", "ctx"), None),
        ),
        check_vma=False,
    )
```

profile of v0, /device:TPU:0, one launch (start us, length us, event | category | flops | bytes accessed | tf_op | source)
XLA Modules:
  0.0 413.0 jit_solution(4538042132011072606)
XLA Ops:
  13.6 4.6 %reduce = bf16[512,640]{1,0:T(8,128)(2,1)S(1)} reduce(bf16[512,1,640]{2,1,0:T(2,128)(2,1)S(1)} %bitcast.141, bf16[]{:T(256)} %broadcast.401), dimensions={1}, to_apply=%bitcast.105.reduce_sub_computation | reduce | bytes 1310722
  19.3 7.3 %all-to-all-start = ((bf16[8,2,20480]{2,1,0:T(2,128)(2,1)}), bf16[8,2,20480]{2,1,0:T(2,128)(2,1)S(1)}, u32[]{:S(2)}, u32[]{:S(2)}) async-start(bf16[8,2,20480]{2,1,0:T(2,128)(2,1)} %reshape.329), calls=%async_computation | async-start | bytes 1310720 | tf_op jit(solution)/shard_map/all_to_all | solution.py:72
  26.8 17.1 %all-to-all-done = bf16[8,2,20480]{2,1,0:T(2,128)(2,1)S(1)} async-done(((bf16[8,2,20480]{2,1,0:T(2,128)(2,1)}), bf16[8,2,20480]{2,1,0:T(2,128)(2,1)S(1)}, u32[]{:S(2)}, u32[]{:S(2)}) %all-to-all-start) | async-done | bytes 655392 | tf_op jit(solution)/shard_map/all_to_all | solution.py:72
  47.9 3.6 all-to-all-start.1
  52.9 30.2 %all-to-all-done.1 = f32[8,64,640]{2,1,0:T(8,128)S(1)} async-done(((f32[8,64,640]{2,1,0:T(8,128)}), f32[8,64,640]{2,1,0:T(8,128)S(1)}, u32[]{:S(2)}, u32[]{:S(2)}) %all-to-all-start.1) | async-done | bytes 1310752 | tf_op jit(solution)/shard_map/all_to_all | solution.py:81
  83.1 3.9 all-to-all-start.2
  87.3 2.6 fusion.31
  89.9 28.5 %all-to-all-done.2 = f32[8,64,640]{2,1,0:T(8,128)S(1)} async-done(((f32[8,64,640]{2,1,0:T(8,128)}), f32[8,64,640]{2,1,0:T(8,128)S(1)}, u32[]{:S(2)}, u32[]{:S(2)}) %all-to-all-start.2) | async-done | bytes 1310752 | tf_op jit(solution)/shard_map/all_to_all | solution.py:82
  127.1 12.8 %convolution_subtract_fusion.2 = f32[16,32,640]{2,0,1:T(8,128)S(1)} fusion(f32[16,32,640]{2,0,1:T(8,128)S(1)} %fusion.25, f32[32,16,640]{2,0,1:T(8,128)S(1)} %get-tuple-element.28), kind=kOutput, calls=%fused_computation.32 | convolution fusion | flops 63245824 | bytes 3932160 | tf_op jit(solution)/shard_map/kb,abw->akw/dot_general | solution.py:30
  147.5 2.3 fusion.19
  149.9 2.3 fusion.15
  152.3 2.4 convolution_subtract_fusion.1
  154.6 2.7 multiply_subtract_fusion
  157.3 2.4 fusion.13
  165.1 2.2 convolution_add_fusion
  168.6 2.8 copy.121
  171.4 4.1 all-to-all-start.4
  175.5 2.8 copy.119
  178.3 34.6 %all-to-all-done.4 = f32[1,512,768]{2,0,1:T(1,128)S(1)} async-done(((f32[1,512,768]{2,0,1:T(1,128)}), f32[1,512,768]{2,0,1:T(1,128)S(1)}, u32[]{:S(2)}, u32[]{:S(2)}) %all-to-all-start.4) | async-done | bytes 1572896 | tf_op jit(solution)/shard_map/all_to_all | solution.py:98
  212.9 3.6 all-to-all-start.3
  218.9 34.8 %all-to-all-done.3 = f32[1,512,768]{2,0,1:T(1,128)S(1)} async-done(((f32[1,512,768]{2,0,1:T(1,128)}), f32[1,512,768]{2,0,1:T(1,128)S(1)}, u32[]{:S(2)}, u32[]{:S(2)}) %all-to-all-start.3) | async-done | bytes 1572896 | tf_op jit(solution)/shard_map/all_to_all | solution.py:97
  256.5 40.6 %all_to_all.63 = f32[8,64,768]{2,1,0:T(8,128)S(1)} all-to-all(f32[8,64,768]{2,1,0:T(8,128)S(1)} %copy.123), channel_id=1, replica_groups=mesh['groups'=2,'ctx'=8,'dp'=2] {'ctx'}, dimensions={0} | all-to-all | bytes 3145728 | tf_op jit(solution)/shard_map/all_to_all | solution.py:102
  305.0 75.9 %all-reduce.5.cloned.1.call-done = f32[3,256,256]{2,0,1:T(4,128)} async-done(((f32[3,256,256]{2,0,1:T(4,128)}), f32[3,256,256]{2,0,1:T(4,128)}) %all-reduce.5.cloned.1.call-update) | async-done | bytes 786448
  383.7 18.9 %all-reduce.7.cloned.1.call-done = (f32[3,32,256]{2,0,1:T(4,128)}, f32[512,256]{1,0:T(8,128)}) async-done(((f32[3,32,256]{2,0,1:T(4,128)}, f32[512,256]{1,0:T(8,128)}), (f32[3,32,256]{2,0,1:T(4,128)}, f32[512,256]{1,0:T(8,128)})) %all-reduce.7.cloned.1.call-update) | async-done | bytes 622608 | tf_op jit(solution)/shard_map/psum | solution.py:174
  (88 shorter events, 54.6 us)
Async XLA Ops:
  7.2 1.1 copy-start
  7.2 3.7 copy-start.5
  7.2 3.7 copy-start.9
  9.5 1.3 copy-start.2
  19.3 24.6 %all-to-all-start = ((bf16[8,2,20480]{2,1,0:T(2,128)(2,1)}), bf16[8,2,20480]{2,1,0:T(2,128)(2,1)S(1)}, u32[]{:S(2)}, u32[]{:S(2)}) async-start(bf16[8,2,20480]{2,1,0:T(2,128)(2,1)} %reshape.329), calls=%async_computation | async-start | bytes 1310720 | tf_op jit(solution)/shard_map/all_to_all | solution.py:72
  47.9 35.2 %all-to-all-start.1 = ((f32[8,64,640]{2,1,0:T(8,128)}), f32[8,64,640]{2,1,0:T(8,128)S(1)}, u32[]{:S(2)}, u32[]{:S(2)}) async-start(f32[8,64,640]{2,1,0:T(8,128)} %copy.97), calls=%async_computation.1 | async-start | bytes 2621440 | tf_op jit(solution)/shard_map/all_to_all | solution.py:81
  83.1 35.2 %all-to-all-start.2 = ((f32[8,64,640]{2,1,0:T(8,128)}), f32[8,64,640]{2,1,0:T(8,128)S(1)}, u32[]{:S(2)}, u32[]{:S(2)}) async-start(f32[8,64,640]{2,1,0:T(8,128)} %copy.99), calls=%async_computation.2 | async-start | bytes 2621440 | tf_op jit(solution)/shard_map/all_to_all | solution.py:82
  118.3 1.6 copy-start.1
  171.4 41.5 %all-to-all-start.4 = ((f32[1,512,768]{2,0,1:T(1,128)}), f32[1,512,768]{2,0,1:T(1,128)S(1)}, u32[]{:S(2)}, u32[]{:S(2)}) async-start(f32[1,512,768]{2,0,1:T(1,128)} %copy.121), calls=%async_computation.4 | async-start | bytes 3145728 | tf_op jit(solution)/shard_map/all_to_all | solution.py:98
  212.9 40.8 %all-to-all-start.3 = ((f32[1,512,768]{2,0,1:T(1,128)}), f32[1,512,768]{2,0,1:T(1,128)S(1)}, u32[]{:S(2)}, u32[]{:S(2)}) async-start(f32[1,512,768]{2,0,1:T(1,128)} %copy.119), calls=%async_computation.3 | async-start | bytes 3145728 | tf_op jit(solution)/shard_map/all_to_all | solution.py:97
  216.5 164.3 %all-reduce.5.cloned.1.call-start = ((), (), s32[]{:S(2)}) async-start(), calls=%async_computation.6 | async-start | bytes 2097152
  298.3 2.3 copy-start.3
  299.3 2.6 copy-start.4
  300.6 1.6 copy-start.6
  302.3 1.4 copy-start.10
  302.3 80.1 %copy-start.7 = (bf16[256,256]{1,0:T(8,128)(2,1)S(1)}, bf16[256,256]{1,0:T(8,128)(2,1)}, u32[]{:S(2)}) copy-start(bf16[256,256]{1,0:T(8,128)(2,1)} %param.7) | copy-start | bytes 393220
  303.6 79.1 %copy-start.8 = (bf16[256,256]{1,0:T(8,128)(2,1)S(1)}, bf16[256,256]{1,0:T(8,128)(2,1)}, u32[]{:S(2)}) copy-start(bf16[256,256]{1,0:T(8,128)(2,1)} %param.8) | copy-start | bytes 393220
  303.7 98.9 %all-reduce.7.cloned.1.call-start = ((), (), s32[]{:S(2)}) async-start(), calls=%async_computation.7 | async-start | bytes 1310720 | tf_op jit(solution)/shard_map/psum | solution.py:174
Sparse Core Ops, SparseCore 0:
  303.8 77.0 all-reduce.4
  383.9 18.5 all-reduce.6
where the time goes:
time: 420 us; the launch traced here: 413 us
  waiting for transfers between devices  240 us (57%)
  matrix products  58.3 us (14%)
  blocking collectives  44.9 us (11%)
  local copies, waits for them, and re-layouts  24.5 us (6%)
  starting transfers between devices  22.6 us (5%)
  between operations  15.4 us (4%)
  other arithmetic  7.2 us (2%)
    unnamed x3, waiting for transfers between devices  75.9 us
    all_to_all x1, blocking collectives, inverse_transform(): lax.all_to_all(rows_part, 'ctx', split_axis=0, concat_axis=1, tiled=True)  40.6 us
    all_to_all x1, waiting for transfers between devices, inverse_transform(): lax.all_to_all(real_part[None], 'ctx', split_axis=1, concat_axis=0, tiled...  34.8 us
    all_to_all x1, waiting for transfers between devices, inverse_transform(): lax.all_to_all(imag_part[None], 'ctx', split_axis=1, concat_axis=0, tiled...  34.6 us
    all_to_all x1, waiting for transfers between devices, forward_transform(): lax.all_to_all(real_part, 'ctx', split_axis=0, concat_axis=1, tiled=True)  30.2 us
    all_to_all x1, waiting for transfers between devices, forward_transform(): lax.all_to_all(imag_part, 'ctx', split_axis=0, concat_axis=1, tiled=True)  28.5 us
    dot_general x8, matrix products, apply_middle(): jnp.einsum('kb,abw->akw', matrix, field, precision=lax.Precision.HIGHEST)  27.4 us
    dot_general x12, matrix products, apply_left(): jnp.tensordot(matrix, field, axes=(1, 0), precision=lax.Precision.HIGHEST)  23.7 us
  transfers between devices with their start and end apart: 7, of which 7 were waited for; matrix products, arithmetic and copies ran while one was open for 3% of the time, Pallas kernels for 0%

commit v1 on v0

--- a/solution.py
+++ b/solution.py
@@ -1,8 +1,20 @@
+import functools
 import math
 import jax
 import jax.numpy as jnp
 from jax import lax
 from jax.sharding import PartitionSpec as P
+
+
+def yards_test(z_in, mesh_ax):
+    v_now = lax.psum(1, mesh_ax)
+    s_next = jnp.split(z_in, v_now, 1)
+    shaped = jnp.stack(s_next)
+    taken_in = lax.all_to_all(shaped, axis_name=mesh_ax, split_axis=0, concat_axis=0)
+    return jnp.concatenate(taken_in, 0)
+
+
+_fix_sections = functools.partial(yards_test, mesh_ax="ctx")
 
 
 def phase_table(left, right, modulus, sign):
@@ -95,7 +107,7 @@
     real_part, imag_part = rotate(real_part, imag_part, jnp.cos(phase), jnp.sin(phase))
     real_part, imag_part = (
         lax.all_to_all(real_part[None], "ctx", split_axis=1, concat_axis=0, tiled=True),
-        lax.all_to_all(imag_part[None], "ctx", split_axis=1, concat_axis=0, tiled=True),
+        _fix_sections(imag_part[None]),
     )
     cos_table, sin_table = dft_matrix(count, 1.0)
     rows_part = apply_left(cos_table, real_part) - apply_left(sin_table, imag_part)

time: 420 us -> 423 us (level)
    unnamed x34 -> x42, local copies, waits for them, and re-layouts: 9.51 us -> 14.3 us
where the time goes in v1:
time: 423 us; the launch traced here: 416 us
  waiting for transfers between devices  239 us (57%)
  matrix products  59.5 us (14%)
  blocking collectives  44.9 us (11%)
  local copies, waits for them, and re-layouts  27.2 us (6%)
  starting transfers between devices  22.4 us (5%)
  between operations  15.7 us (4%)
  other arithmetic  7.19 us (2%)
    unnamed x3, waiting for transfers between devices  75.9 us
    all_to_all x1, blocking collectives, inverse_transform(): lax.all_to_all(rows_part, 'ctx', split_axis=0, concat_axis=1, tiled=True)  40.6 us
    all_to_all x1, waiting for transfers between devices, yards_test(): lax.all_to_all(shaped, axis_name=mesh_ax, split_axis=0, concat_axis=0)  34.6 us
    all_to_all x1, waiting for transfers between devices, inverse_transform(): lax.all_to_all(real_part[None], 'ctx', split_axis=1, concat_axis=0, tiled...  33.6 us
    all_to_all x1, waiting for transfers between devices, forward_transform(): lax.all_to_all(real_part, 'ctx', split_axis=0, concat_axis=1, tiled=True)  30.3 us
    all_to_all x1, waiting for transfers between devices, forward_transform(): lax.all_to_all(imag_part, 'ctx', split_axis=0, concat_axis=1, tiled=True)  28.5 us
    dot_general x8, matrix products, apply_middle(): jnp.einsum('kb,abw->akw', matrix, field, precision=lax.Precision.HIGHEST)  27.4 us
    dot_general x12, matrix products, apply_left(): jnp.tensordot(matrix, field, axes=(1, 0), precision=lax.Precision.HIGHEST)  24.8 us
  transfers between devices with their start and end apart: 7, of which 7 were waited for; matrix products, arithmetic and copies ran while one was open for 3% of the time, Pallas kernels for 0%

profile of v1, /device:TPU:0, one launch (start us, length us, event | category | flops | bytes accessed | tf_op | source)
XLA Modules:
  0.0 415.7 jit_solution(12246677001142174243)
XLA Ops:
  13.6 4.6 %reduce = bf16[512,640]{1,0:T(8,128)(2,1)S(1)} reduce(bf16[512,1,640]{2,1,0:T(2,128)(2,1)S(1)} %bitcast.174, bf16[]{:T(256)} %broadcast.401), dimensions={1}, to_apply=%bitcast.139.reduce_sub_computation | reduce | bytes 1310722
  19.3 7.3 %all-to-all-start = ((bf16[8,2,20480]{2,1,0:T(2,128)(2,1)}), bf16[8,2,20480]{2,1,0:T(2,128)(2,1)S(1)}, u32[]{:S(2)}, u32[]{:S(2)}) async-start(bf16[8,2,20480]{2,1,0:T(2,128)(2,1)} %reshape.330), calls=%async_computation | async-start | bytes 1310720 | tf_op jit(solution)/shard_map/all_to_all | solution.py:84
  26.8 17.1 %all-to-all-done = bf16[8,2,20480]{2,1,0:T(2,128)(2,1)S(1)} async-done(((bf16[8,2,20480]{2,1,0:T(2,128)(2,1)}), bf16[8,2,20480]{2,1,0:T(2,128)(2,1)S(1)}, u32[]{:S(2)}, u32[]{:S(2)}) %all-to-all-start) | async-done | bytes 655392 | tf_op jit(solution)/shard_map/all_to_all | solution.py:84
  48.0 3.6 all-to-all-start.1
  52.9 30.3 %all-to-all-done.1 = f32[8,64,640]{2,1,0:T(8,128)S(1)} async-done(((f32[8,64,640]{2,1,0:T(8,128)}), f32[8,64,640]{2,1,0:T(8,128)S(1)}, u32[]{:S(2)}, u32[]{:S(2)}) %all-to-all-start.1) | async-done | bytes 1310752 | tf_op jit(solution)/shard_map/all_to_all | solution.py:93
  83.2 3.9 all-to-all-start.2
  87.2 2.6 fusion.32
  89.8 28.5 %all-to-all-done.2 = f32[8,64,640]{2,1,0:T(8,128)S(1)} async-done(((f32[8,64,640]{2,1,0:T(8,128)}), f32[8,64,640]{2,1,0:T(8,128)S(1)}, u32[]{:S(2)}, u32[]{:S(2)}) %all-to-all-start.2) | async-done | bytes 1310752 | tf_op jit(solution)/shard_map/all_to_all | solution.py:94
  127.1 12.7 %convolution_subtract_fusion.2 = f32[16,32,640]{2,0,1:T(8,128)S(1)} fusion(f32[16,32,640]{2,0,1:T(8,128)S(1)} %fusion.26, f32[32,16,640]{2,0,1:T(8,128)S(1)} %get-tuple-element.31), kind=kOutput, calls=%fused_computation.33 | convolution fusion | flops 63245824 | bytes 3932160 | tf_op jit(solution)/shard_map/kb,abw->akw/dot_general | solution.py:42
  147.5 2.3 fusion.20
  149.9 2.3 fusion.16
  152.2 2.4 convolution_subtract_fusion.1
  154.6 2.7 multiply_subtract_fusion
  157.3 2.4 fusion.14
  165.1 2.3 convolution_add_fusion
  174.2 3.6 all-to-all-start.4
  177.9 2.8 copy.154
  180.7 34.6 %all-to-all-done.4 = f32[8,1,64,768]{3,2,1,0:T(8,128)S(1)} async-done(((f32[8,1,64,768]{3,2,1,0:T(8,128)}), f32[8,1,64,768]{3,2,1,0:T(8,128)S(1)}, u32[]{:S(2)}, u32[]{:S(2)}) %all-to-all-start.4) | async-done | bytes 1572896 | tf_op jit(solution)/shard_map/all_to_all | solution.py:13
  215.3 3.6 all-to-all-start.3
  219.2 3.3 fusion
  222.6 33.6 %all-to-all-done.3 = f32[1,512,768]{2,0,1:T(1,128)S(1)} async-done(((f32[1,512,768]{2,0,1:T(1,128)}), f32[1,512,768]{2,0,1:T(1,128)S(1)}, u32[]{:S(2)}, u32[]{:S(2)}) %all-to-all-start.3) | async-done | bytes 1572896 | tf_op jit(solution)/shard_map/all_to_all | solution.py:109
  258.9 40.6 %all_to_all.56 = f32[8,64,768]{2,1,0:T(8,128)S(1)} all-to-all(f32[8,64,768]{2,1,0:T(8,128)S(1)} %copy.157), channel_id=1, replica_groups=mesh['groups'=2,'ctx'=8,'dp'=2] {'ctx'}, dimensions={0} | all-to-all | bytes 3145728 | tf_op jit(solution)/shard_map/all_to_all | solution.py:114
  307.4 75.9 %all-reduce.5.cloned.1.call-done = f32[3,256,256]{2,0,1:T(4,128)} async-done(((f32[3,256,256]{2,0,1:T(4,128)}), f32[3,256,256]{2,0,1:T(4,128)}) %all-reduce.5.cloned.1.call-update) | async-done | bytes 786448
  386.1 18.8 %all-reduce.7.cloned.1.call-done = (f32[3,32,256]{2,0,1:T(4,128)}, f32[512,256]{1,0:T(8,128)}) async-done(((f32[3,32,256]{2,0,1:T(4,128)}, f32[512,256]{1,0:T(8,128)}), (f32[3,32,256]{2,0,1:T(4,128)}, f32[512,256]{1,0:T(8,128)})) %all-reduce.7.cloned.1.call-update) | async-done | bytes 622608 | tf_op jit(solution)/shard_map/psum | solution.py:186
  (96 shorter events, 58.2 us)
Async XLA Ops:
  7.2 1.1 copy-start
  7.2 3.7 copy-start.6
  7.2 3.7 copy-start.10
  9.5 1.3 copy-start.3
  19.3 24.6 %all-to-all-start = ((bf16[8,2,20480]{2,1,0:T(2,128)(2,1)}), bf16[8,2,20480]{2,1,0:T(2,128)(2,1)S(1)}, u32[]{:S(2)}, u32[]{:S(2)}) async-start(bf16[8,2,20480]{2,1,0:T(2,128)(2,1)} %reshape.330), calls=%async_computation | async-start | bytes 1310720 | tf_op jit(solution)/shard_map/all_to_all | solution.py:84
  48.0 35.2 %all-to-all-start.1 = ((f32[8,64,640]{2,1,0:T(8,128)}), f32[8,64,640]{2,1,0:T(8,128)S(1)}, u32[]{:S(2)}, u32[]{:S(2)}) async-start(f32[8,64,640]{2,1,0:T(8,128)} %copy.132), calls=%async_computation.1 | async-start | bytes 2621440 | tf_op jit(solution)/shard_map/all_to_all | solution.py:93
  83.2 35.2 %all-to-all-start.2 = ((f32[8,64,640]{2,1,0:T(8,128)}), f32[8,64,640]{2,1,0:T(8,128)S(1)}, u32[]{:S(2)}, u32[]{:S(2)}) async-start(f32[8,64,640]{2,1,0:T(8,128)} %copy.134), calls=%async_computation.2 | async-start | bytes 2621440 | tf_op jit(solution)/shard_map/all_to_all | solution.py:94
  118.4 1.6 copy-start.2
  174.2 41.1 %all-to-all-start.4 = ((f32[8,1,64,768]{3,2,1,0:T(8,128)}), f32[8,1,64,768]{3,2,1,0:T(8,128)S(1)}, u32[]{:S(2)}, u32[]{:S(2)}) async-start(f32[8,1,64,768]{3,2,1,0:T(8,128)} %fusion.48), calls=%async_computation.4 | async-start | bytes 3145728 | tf_op jit(solution)/shard_map/all_to_all | solution.py:13
  215.3 40.8 %all-to-all-start.3 = ((f32[1,512,768]{2,0,1:T(1,128)}), f32[1,512,768]{2,0,1:T(1,128)S(1)}, u32[]{:S(2)}, u32[]{:S(2)}) async-start(f32[1,512,768]{2,0,1:T(1,128)} %copy.154), calls=%async_computation.3 | async-start | bytes 3145728 | tf_op jit(solution)/shard_map/all_to_all | solution.py:109
  218.9 164.3 %all-reduce.5.cloned.1.call-start = ((), (), s32[]{:S(2)}) async-start(), calls=%async_computation.6 | async-start | bytes 2097152
  222.6 33.7 %copy-start.1 = (f32[8,64,768]{2,0,1:T(8,128)S(1)}, f32[8,64,768]{2,0,1:T(8,128)}, u32[]{:S(2)}) copy-start(f32[8,64,768]{2,0,1:T(8,128)} %fusion) | copy-start | bytes 4718596
  300.7 2.3 copy-start.4
  301.7 2.6 copy-start.5
  303.0 1.6 copy-start.7
  304.7 1.4 copy-start.11
  304.7 80.1 %copy-start.8 = (bf16[256,256]{1,0:T(8,128)(2,1)S(1)}, bf16[256,256]{1,0:T(8,128)(2,1)}, u32[]{:S(2)}) copy-start(bf16[256,256]{1,0:T(8,128)(2,1)} %param.7) | copy-start | bytes 393220
  306.1 79.1 %copy-start.9 = (bf16[256,256]{1,0:T(8,128)(2,1)S(1)}, bf16[256,256]{1,0:T(8,128)(2,1)}, u32[]{:S(2)}) copy-start(bf16[256,256]{1,0:T(8,128)(2,1)} %param.8) | copy-start | bytes 393220
  306.1 98.9 %all-reduce.7.cloned.1.call-start = ((), (), s32[]{:S(2)}) async-start(), calls=%async_computation.7 | async-start | bytes 1310720 | tf_op jit(solution)/shard_map/psum | solution.py:186
Sparse Core Ops, SparseCore 0:
  306.2 77.0 all-reduce.4
  386.3 18.5 all-reduce.6
